TPU v7x, 32 devices: a whole 2x2x4 slice. The times are simulated.
32 devices in a mesh: seq: 8 (over z, x), head: 4 (over y, core).
Axes of the slice: x: 2, y: 2, z: 4, core: 2. Of those that a mesh axis runs over, the one named last changes fastest.
Arguments:
- features_in: bfloat16 [4096, 3072], P('seq', 'head'), may hold values from -66 to 66
- gate_in: bfloat16 [4096, 3072], P('seq', 'head'), may hold values from -6 to 6
- b_input: bfloat16 [4096, 128], P('seq'), may hold values from -0.0234375 to 0.0234375
- c_input: bfloat16 [4096, 128], P('seq'), may hold values from -6 to 6
- log_decay: bfloat16 [4096, 48], P('seq', 'head'), may hold values from -1 to 0, as said below
- row_target: int32 [4096], P('seq'), may hold values from 0 to 4095, as said below
- doc_lengths: int32 [4], replicated, may hold values from 1 to 2048, 4096 in all
- skip_gain: float32 [48], P('head'), may hold values from 0.5 to 1.5
- norm_gain: float32 [3072], P('head'), may hold values from 0.1 to 1.9
- out_weight: bfloat16 [3072, 1536], P('head'), may hold values from -0.109375 to 0.109375
Outputs:
- layer_out: bfloat16 [4096, 1536], P(('seq', 'head'))
Inputs may be any that keep to these rules, and one draw needn't show every extreme that they name: row_target is a permutation; the rows of one device go to every device along seq, exactly 64 rows to each. `doc_lengths`: the lengths sum to 4096. `log_decay`: every decay is below one.
All inputs are finite; a program needn't handle non-finite values.
Results may differ from a plain program's by a relative error of at most 0.022.
Values may be sent and summed in bfloat16 or wider, within the bound.
A program may use at most 128 MiB of HBM per device.

v0:
```python
import jax
import jax.numpy as jnp
from jax import lax
from jax.sharding import PartitionSpec as P

ATTENTION_LANES = 48
HEAD_DIM = 64
BLOCK = 512


far_below = -1e30
norm_eps = 1e-05


def prefix(x, axis, combine, identity):
    length, here = (lax.axis_size(axis), lax.axis_index(axis))
    everything = jax.tree.map(
        lambda part, kind: lax.all_gather(part.astype(kind), axis), x, (jnp.bfloat16, jnp.bfloat16)
    )
    start = jax.tree.map(
        lambda part, zero: jnp.broadcast_to(jnp.asarray(zero, part.dtype), part.shape), x, identity
    )

    def hop(k, before):
        reached = k < here
        new = combine(
            before, jax.tree.map(lambda part, own: part[k].astype(own.dtype), everything, x)
        )
        return jax.tree.map(lambda a, b: jnp.where(reached, a, b), new, before)

    return lax.fori_loop(0, length, hop, start)


def doc_index(places, starts):
    return jnp.sum((starts[None, :] <= places[:, None]).astype(jnp.int32), axis=1) - 1


def state_terms(by_head, key_block, decay_block, doc_block, before):
    running = jnp.cumsum(decay_block.astype(jnp.float32), axis=0)
    same_doc = (doc_block == doc_block[-1]).astype(jnp.float32)
    closing_weight = jnp.exp(running[-1][None, :] - running) * same_doc[:, None]
    weighted = (key_block.astype(jnp.float32)[None, :, :] * closing_weight.T[:, :, None]).astype(
        jnp.bfloat16
    )
    block_state = jnp.einsum("hsn,shp->hpn", weighted, by_head, preferred_element_type=jnp.float32)
    through = jnp.exp(running[-1]) * (doc_block[-1] == before).astype(jnp.float32)
    return (block_state, through, running)


def inner_terms(by_head, key_block, query_block, running, doc_block):
    length = running.shape[0]
    later = lax.broadcasted_iota(jnp.int32, (length, length), 0)
    earlier = lax.broadcasted_iota(jnp.int32, (length, length), 1)
    allowed = (later >= earlier) & (doc_block[:, None] == doc_block[None, :])
    running_heads = running.T
    decay_gaps = jnp.where(
        allowed[None, :, :], running_heads[:, :, None] - running_heads[:, None, :], far_below
    )
    products = jnp.einsum("tn,sn->ts", query_block, key_block, preferred_element_type=jnp.float32)
    affinity_logits = (products[None, :, :] * jnp.exp(decay_gaps)).astype(jnp.bfloat16)
    return jnp.einsum("hts,shp->thp", affinity_logits, by_head, preferred_element_type=jnp.float32)


def entry_terms(query_block, carry_state, running, doc_block, before):
    entry_weight = jnp.exp(running) * (doc_block == before).astype(jnp.float32)[:, None]
    carried = jnp.einsum(
        "tn,hpn->thp", query_block.astype(jnp.float32), carry_state, precision=lax.Precision.HIGHEST
    )
    return carried * entry_weight[:, :, None]


def combine(earlier, later):
    return (earlier[0] * later[0], later[0][:, None, None] * earlier[1] + later[1])


def body(
    features_in,
    gate_in,
    b_input,
    c_input,
    log_decay,
    row_target,
    doc_lengths,
    skip_gain,
    norm_gain,
    out_weight,
):
    tok_dev = features_in.shape[0]
    heads_here = log_decay.shape[1]
    width = features_in.shape[1] // heads_here
    shards = lax.axis_size("seq")
    capacity = tok_dev // shards
    owner = row_target // tok_dev
    local_place = row_target - owner * tok_dev
    owner_hits = (owner[:, None] == lax.broadcasted_iota(jnp.int32, (tok_dev, shards), 1)).astype(
        jnp.int32
    )
    slot_rank = jnp.sum((jnp.cumsum(owner_hits, axis=0) - owner_hits) * owner_hits, axis=1)
    slot_index = owner * capacity + slot_rank

    def pack_rows(values):
        blank = jnp.zeros((shards * capacity,) + values.shape[1:], values.dtype)
        return blank.at[slot_index].set(values).reshape((shards, capacity) + values.shape[1:])

    slot_place = (
        jnp.full((shards * capacity,), tok_dev, jnp.int32)
        .at[slot_index]
        .set(local_place)
        .reshape(shards, capacity)
    )
    moved_inputs, gate_early, moved_keys, moved_queries, moved_decay, moved_place = (
        lax.all_to_all(pack_rows(features_in), "seq", split_axis=0, concat_axis=0, tiled=True),
        lax.all_to_all(pack_rows(gate_in), "seq", split_axis=0, concat_axis=0, tiled=True),
        lax.all_to_all(pack_rows(b_input), "seq", split_axis=0, concat_axis=0, tiled=True),
        lax.all_to_all(pack_rows(c_input), "seq", split_axis=0, concat_axis=0, tiled=True),
        lax.all_to_all(pack_rows(log_decay), "seq", split_axis=0, concat_axis=0, tiled=True),
        lax.all_to_all(slot_place, "seq", split_axis=0, concat_axis=0, tiled=True),
    )
    arrived = moved_place.reshape(shards * capacity)

    def unpack_rows(values):
        flattened = values.reshape((shards * capacity,) + values.shape[2:])
        blank = jnp.zeros((tok_dev,) + values.shape[2:], values.dtype)
        return blank.at[arrived].set(flattened, mode="drop")

    features = unpack_rows(moved_inputs)
    key_rows = unpack_rows(moved_keys)
    query_rows = unpack_rows(moved_queries)
    decays = unpack_rows(moved_decay)
    key_full, query_full = (key_rows, query_rows)
    doc_starts = jnp.cumsum(doc_lengths) - doc_lengths
    first_place = lax.axis_index("seq") * tok_dev
    blocks = tok_dev // BLOCK
    places = first_place + lax.broadcasted_iota(jnp.int32, (tok_dev,), 0)
    doc_ids = doc_index(places, doc_starts).reshape(blocks, BLOCK)
    doc_before = doc_index(
        first_place + lax.broadcasted_iota(jnp.int32, (blocks,), 0) * BLOCK - 1, doc_starts
    )
    inputs_blocks = features.reshape(blocks, BLOCK, heads_here, width)
    key_blocks = key_full.reshape(blocks, BLOCK, key_full.shape[1])
    query_blocks = query_full.reshape(blocks, BLOCK, query_full.shape[1])
    decay_blocks = decays.reshape(blocks, BLOCK, heads_here)

    def state_pass(carry, pieces):
        carry_state, kept_share = carry
        by_head, key_block, query_block, decay_block, doc_block, before = pieces
        block_state, through, running = state_terms(
            by_head, key_block, decay_block, doc_block, before
        )
        new_carry = (through[:, None, None] * carry_state + block_state, through * kept_share)
        return (new_carry, (block_state, through, running))

    zero_state = jnp.zeros((heads_here, width, key_full.shape[1]), jnp.float32)
    ones_here = jnp.ones((heads_here,), jnp.float32)
    local_carry, block_outputs = lax.scan(
        state_pass,
        (zero_state, ones_here),
        (inputs_blocks, key_blocks, query_blocks, decay_blocks, doc_ids, doc_before),
    )
    local_state, local_kept = local_carry
    block_states, throughs, runnings = (block_outputs[0], block_outputs[1], block_outputs[2])
    entry_kept, entry_state = prefix(
        (local_kept, local_state), "seq", combine, (ones_here, zero_state)
    )

    def mix_pass(carry_state, pieces):
        by_head, key_block, query_block, running, doc_block, before, block_state, through = pieces
        carried = entry_terms(query_block, carry_state, running, doc_block, before)
        mixed_block = (
            inner_terms(by_head, key_block, query_block, running, doc_block)
            + carried
            + skip_gain[None, :, None] * by_head.astype(jnp.float32)
        )
        return (through[:, None, None] * carry_state + block_state, mixed_block)

    final_state, mixed = lax.scan(
        mix_pass,
        entry_state,
        (
            inputs_blocks,
            key_blocks,
            query_blocks,
            runnings,
            doc_ids,
            doc_before,
            block_states,
            throughs,
        ),
    )
    mixed = mixed.reshape(tok_dev, heads_here * width)
    gate_rows = unpack_rows(gate_early)
    gated = mixed * jax.nn.silu(gate_rows.astype(jnp.float32))
    squares = lax.psum(jnp.sum(gated * gated, axis=1), "head")
    row_scale = lax.rsqrt(squares / (ATTENTION_LANES * HEAD_DIM) + norm_eps)
    normed = (gated * row_scale[:, None] * norm_gain[None, :]).astype(jnp.bfloat16)
    return lax.psum_scatter(
        jnp.dot(normed, out_weight, preferred_element_type=jnp.float32).astype(jnp.bfloat16),
        "head",
        scatter_dimension=0,
        tiled=True,
    )


def solution(mesh):
    in_specs = (
        P("seq", "head"),
        P("seq", "head"),
        P("seq", None),
        P("seq", None),
        P("seq", "head"),
        P("seq"),
        P(),
        P("head"),
        P("head"),
        P("head", None),
    )
    out_specs = P(("seq", "head"), None)
    return jax.shard_map(body, mesh=mesh, in_specs=in_specs, out_specs=out_specs, check_vma=False)
```

profile of v0, /device:TPU:27, one launch (start us, length us, event | category | flops | bytes accessed | tf_op | source)
XLA Modules:
  0.0 209.7 jit_solution(2486592667774685424)
XLA Ops:
  8.9 2.4 %scatter_custom_fusion = s32[512]{0:T(512)S(1)} fusion(s32[512]{0:T(512)S(1)} %compare_select_fusion.1, s32[512]{0:T(512)S(1)} %get-tuple-element.199, s32[]{:T(128)} %constant.111.clone.1), kind=kCustom, calls=%fused_computation.91 | custom fusion | bytes 2052 | tf_op jit(solution)/shard_map/scatter | solution.py:108
  12.0 5.4 %all-to-all-start = ((s32[8,1,64]{2,1,0:T(1,128)}), s32[8,1,64]{2,1,0:T(1,128)S(1)}, u32[]{:S(2)}, u32[]{:S(2)}) async-start(s32[8,1,64]{2,1,0:T(1,128)} %all_to_all.21), calls=%async_computation | async-start | bytes 8192 | tf_op jit(solution)/shard_map/all_to_all | solution.py:117
  18.3 1.8 scatter_custom_fusion.7
  20.9 5.4 %all-to-all-start.4 = ((bf16[8,2,384]{2,1,0:T(2,128)(2,1)}), bf16[8,2,384]{2,1,0:T(2,128)(2,1)S(1)}, u32[]{:S(2)}, u32[]{:S(2)}) async-start(bf16[8,2,384]{2,1,0:T(2,128)(2,1)} %reshape.385), calls=%async_computation.4 | async-start | bytes 24576 | tf_op jit(solution)/shard_map/all_to_all | solution.py:116
  27.2 2.7 %scatter_custom_fusion.5 = bf16[512,128]{1,0:T(8,128)(2,1)} fusion(s32[512]{0:T(512)S(1)} %compare_select_fusion.1, bf16[512,128]{1,0:T(8,128)(2,1)} %param.14, bf16[]{:T(256)} %constant.110.clone.1), kind=kCustom, calls=%fused_computation.53 | custom fusion | bytes 131584 | tf_op jit(solution)/shard_map/scatter | solution.py:103
  29.9 5.4 %all-to-all-start.3 = ((bf16[8,64,128]{2,1,0:T(8,128)(2,1)}), bf16[8,64,128]{2,1,0:T(8,128)(2,1)S(1)}, u32[]{:S(2)}, u32[]{:S(2)}) async-start(bf16[8,64,128]{2,1,0:T(8,128)(2,1)} %bitcast.9), calls=%async_computation.3 | async-start | bytes 262144 | tf_op jit(solution)/shard_map/all_to_all | solution.py:114
  35.3 1.4 fusion.45
  36.7 4.1 %scatter_custom_fusion.1 = bf16[512,768]{1,0:T(8,128)(2,1)} fusion(s32[512]{0:T(512)S(1)} %compare_select_fusion.1, bf16[512,768]{1,0:T(8,128)(2,1)} %param.12, bf16[]{:T(256)} %constant.110.clone.1), kind=kCustom, calls=%fused_computation.44 | custom fusion | bytes 786944 | tf_op jit(solution)/shard_map/scatter | solution.py:103
  40.9 5.4 %all-to-all-start.1 = ((bf16[8,64,768]{2,1,0:T(8,128)(2,1)}), bf16[8,64,768]{2,1,0:T(8,128)(2,1)S(1)}, u32[]{:S(2)}, u32[]{:S(2)}) async-start(bf16[8,64,768]{2,1,0:T(8,128)(2,1)} %bitcast.4), calls=%async_computation.1 | async-start | bytes 1572864 | tf_op jit(solution)/shard_map/all_to_all | solution.py:112
  50.6 1.8 scatter_custom_fusion.8
  54.6 2.3 %scatter_custom_fusion.6 = bf16[512,128]{1,0:T(8,128)(2,1)S(1)} fusion(s32[512]{0:T(512)} %bitcast.90, bf16[512,128]{1,0:T(8,128)(2,1)} %bitcast.84, bf16[]{:T(256)} %constant.110.clone.1), kind=kCustom, calls=%fused_computation.51 | custom fusion | bytes 131584 | tf_op jit(solution)/shard_map/scatter | solution.py:124
  57.6 6.0 %all-to-all-done.1 = bf16[8,64,768]{2,1,0:T(8,128)(2,1)S(1)} async-done(((bf16[8,64,768]{2,1,0:T(8,128)(2,1)}), bf16[8,64,768]{2,1,0:T(8,128)(2,1)S(1)}, u32[]{:S(2)}, u32[]{:S(2)}) %all-to-all-start.1) | async-done | bytes 786464 | tf_op jit(solution)/shard_map/all_to_all | solution.py:112
  63.7 3.7 %scatter_custom_fusion.2 = bf16[512,768]{1,0:T(8,128)(2,1)} fusion(s32[512]{0:T(512)} %bitcast.91, bf16[512,768]{1,0:T(8,128)(2,1)S(1)} %bitcast.72, bf16[]{:T(256)} %constant.110.clone.1), kind=kCustom, calls=%fused_computation.42 | custom fusion | bytes 786944 | tf_op jit(solution)/shard_map/scatter | solution.py:124
  67.4 1.5 copy.35
  68.8 2.0 fusion.12
  70.8 2.7 %scatter_custom_fusion.3 = bf16[512,128]{1,0:T(8,128)(2,1)} fusion(s32[512]{0:T(512)S(1)} %compare_select_fusion.1, bf16[512,128]{1,0:T(8,128)(2,1)} %param.15, bf16[]{:T(256)} %constant.110.clone.1), kind=kCustom, calls=%fused_computation.57 | custom fusion | bytes 131584 | tf_op jit(solution)/shard_map/scatter | solution.py:103
  73.5 5.4 %all-to-all-start.2 = ((bf16[8,64,128]{2,1,0:T(8,128)(2,1)}), bf16[8,64,128]{2,1,0:T(8,128)(2,1)S(1)}, u32[]{:S(2)}, u32[]{:S(2)}) async-start(bf16[8,64,128]{2,1,0:T(8,128)(2,1)} %bitcast.7), calls=%async_computation.2 | async-start | bytes 262144 | tf_op jit(solution)/shard_map/all_to_all | solution.py:115
  79.0 4.1 %scatter_custom_fusion.9 = bf16[512,768]{1,0:T(8,128)(2,1)} fusion(s32[512]{0:T(512)S(1)} %compare_select_fusion.1, bf16[512,768]{1,0:T(8,128)(2,1)} %param.13, bf16[]{:T(256)} %constant.110.clone.1), kind=kCustom, calls=%fused_computation.40 | custom fusion | bytes 786944 | tf_op jit(solution)/shard_map/scatter | solution.py:103
  83.1 6.3 %all-to-all-start.5 = ((bf16[8,64,768]{2,1,0:T(8,128)(2,1)}), bf16[8,64,768]{2,1,0:T(8,128)(2,1)}, u32[]{:S(2)}, u32[]{:S(2)}) async-start(bf16[8,64,768]{2,1,0:T(8,128)(2,1)} %bitcast.70), calls=%async_computation.5 | async-start | bytes 1572864 | tf_op jit(solution)/shard_map/all_to_all | solution.py:113
  91.2 30.3 %all-gather.1 = bf16[8,1,12]{2,1,0:T(2,128)(2,1)S(1)} all-gather(bf16[1,1,12]{2,1,0:T(2,128)(2,1)S(1)} %bitcast.88), channel_id=1, replica_groups=mesh['seq'=8,'head'=4] {'seq'}, dimensions={0}, use_global_device_ids=true | all-gather | bytes 216 | tf_op jit(solution)/shard_map/all_gather | solution.py:18
  121.6 1.4 exponential_multiply_fusion
  123.0 2.7 %scatter_custom_fusion.4 = bf16[512,128]{1,0:T(8,128)(2,1)} fusion(s32[512]{0:T(512)} %bitcast.92, bf16[512,128]{1,0:T(8,128)(2,1)} %bitcast.85, bf16[]{:T(256)} %constant.110.clone.1), kind=kCustom, calls=%fused_computation.55 | custom fusion | bytes 131584 | tf_op jit(solution)/shard_map/scatter | solution.py:124
  125.7 2.2 %fusion.48 = f32[512,512]{1,0:T(8,128)} fusion(bf16[512,128]{1,0:T(8,128)(2,1)} %scatter_custom_fusion.4, bf16[512,128]{1,0:T(8,128)(2,1)} %copy-done.2), kind=kOutput, calls=%fused_computation.97 | convolution fusion | flops 67108864 | bytes 1310720 | tf_op jit(solution)/shard_map/while/body/eval_jaxpr/tn,sn->ts/dot_general | solution.py:59
  127.9 4.1 %scatter_custom_fusion.10 = bf16[512,768]{1,0:T(8,128)(2,1)} fusion(s32[512]{0:T(512)} %bitcast.93, bf16[512,768]{1,0:T(8,128)(2,1)} %bitcast.24, bf16[]{:T(256)} %constant.110.clone.1), kind=kCustom, calls=%fused_computation.38 | custom fusion | bytes 786944 | tf_op jit(solution)/shard_map/scatter | solution.py:124
  132.1 5.8 %fusion.1 = f32[12,64,512]{2,1,0:T(8,128)} fusion(bf16[512,12,64]{0,2,1:T(8,128)(2,1)S(1)} %bitcast.68, f32[12,512]{1,0:T(8,128)} %bitcast.79, f32[512,512]{1,0:T(8,128)} %fusion.48, pred[512,512]{1,0:T(8,128)(4,1)} %fusion.13), kind=kOutput, calls=%fused_computation.15 | convolution fusion | flops 415236096 | bytes 3694592 | tf_op jit(solution)/shard_map/while/body/eval_jaxpr/hts,shp->thp/dot_general | solution.py:61
  137.9 8.7 %while.9 = (s32[]{:T(128)}, f32[12,64,128]{2,1,0:T(8,128)S(1)}, s32[]{:T(128)}, bf16[8,12]{1,0:T(8,128)(2,1)S(1)}, bf16[8,12,64,128]{3,2,1,0:T(8,128)(2,1)}, /*index=5*/s32[]{:T(128)}, s32[]{:T(128)}) while((s32[]{:T(128)}, f32[12,64,128]{2,1,0:T(8,128)S(1)}, s32[]{:T(128)}, bf16[8,12]{1,0:T(8,128)(2,1)S(1)}, ...), condition=%wide.region_18.19_spmd.clone, body=%wide.region_17.18_spmd.clone.sunk | while | flops 491536 | bytes 983265 | solution.py:31
  146.6 3.5 %fusion.8 = f32[512,12,64]{0,2,1:T(8,128)} fusion(f32[12,64,512]{2,1,0:T(8,128)} %fusion.1, bf16[512,12,64]{0,2,1:T(8,128)(2,1)S(1)} %bitcast.69, f32[12,64,128]{2,1,0:T(8,128)S(1)} %get-tuple-element.168, f32[12]{0:T(128)S(1)} %copy-done.8, f32[512,12]{0,1:T(8,128)} %exponential_multiply_fusion, bf16[512,128]{1,0:T(8,128)(2,1)} %scatter_custom_fusion.4), kind=kOutput, calls=%fused_computation.27 | convolution fusion | flops 605945856 | bytes 4481072 | tf_op jit(solution)/shard_map/while/body/eval_jaxpr/tn,hpn->thp/dot_general | solution.py:66
  150.1 3.1 %copy.42 = f32[512,768]{1,0:T(8,128)} copy(f32[512,768]{0,1:T(8,128)} %bitcast.66) | data formatting | bytes 3145728 | tf_op jit(solution)/shard_map/reshape | solution.py:190
  153.2 2.0 multiply_reduce_fusion
  155.2 13.9 %psum.7 = f32[512]{0:T(512)S(1)} all-reduce(f32[512]{0:T(512)S(1)} %multiply_reduce_fusion), channel_id=1, replica_groups=mesh['seq'=8,'head'=4] {'head'}, use_global_device_ids=true, to_apply=%region_22.23 | all-reduce | flops 512 | bytes 4096 | tf_op jit(solution)/shard_map/psum | solution.py:193
  169.1 4.3 %convolution_convert_fusion = bf16[512,1536]{1,0:T(8,128)(2,1)} fusion(bf16[768,1536]{1,0:T(8,128)(2,1)S(1)} %copy-done, f32[768]{0:T(1024)S(1)} %copy-done.9, f32[512]{0:T(512)S(1)} %add_rsqrt_fusion, f32[512,768]{1,0:T(8,128)} %copy.42, bf16[512,768]{1,0:T(8,128)(2,1)S(1)} %copy-done.1), kind=kOutput, calls=%fused_computation.18 | convolution fusion | flops 1212284928 | bytes 6296576 | tf_op jit(solution)/shard_map/dot_general | solution.py:197
  173.4 29.5 %reduce-scatter.2.cloned.1.call-done = bf16[128,1536]{1,0:T(8,128)(2,1)} async-done(((bf16[512,1536]{1,0:T(8,128)(2,1)}), bf16[128,1536]{1,0:T(8,128)(2,1)}) %reduce-scatter.2.cloned.1.call-update) | async-done | bytes 393232 | tf_op jit(solution)/shard_map/reduce_scatter | solution.py:196
  (89 shorter events, 21.9 us)
Async XLA Ops:
  6.5 162.5 %copy-start = (bf16[768,1536]{1,0:T(8,128)(2,1)S(1)}, bf16[768,1536]{1,0:T(8,128)(2,1)}, u32[]{:S(2)}) copy-start(bf16[768,1536]{1,0:T(8,128)(2,1)} %param.21) | copy-start | bytes 7077892
  12.0 8.9 %all-to-all-start = ((s32[8,1,64]{2,1,0:T(1,128)}), s32[8,1,64]{2,1,0:T(1,128)S(1)}, u32[]{:S(2)}, u32[]{:S(2)}) async-start(s32[8,1,64]{2,1,0:T(1,128)} %all_to_all.21), calls=%async_computation | async-start | bytes 8192 | tf_op jit(solution)/shard_map/all_to_all | solution.py:117
  20.9 9.0 %all-to-all-start.4 = ((bf16[8,2,384]{2,1,0:T(2,128)(2,1)}), bf16[8,2,384]{2,1,0:T(2,128)(2,1)S(1)}, u32[]{:S(2)}, u32[]{:S(2)}) async-start(bf16[8,2,384]{2,1,0:T(2,128)(2,1)} %reshape.385), calls=%async_computation.4 | async-start | bytes 24576 | tf_op jit(solution)/shard_map/all_to_all | solution.py:116
  29.9 11.0 %all-to-all-start.3 = ((bf16[8,64,128]{2,1,0:T(8,128)(2,1)}), bf16[8,64,128]{2,1,0:T(8,128)(2,1)S(1)}, u32[]{:S(2)}, u32[]{:S(2)}) async-start(bf16[8,64,128]{2,1,0:T(8,128)(2,1)} %bitcast.9), calls=%async_computation.3 | async-start | bytes 262144 | tf_op jit(solution)/shard_map/all_to_all | solution.py:114
  40.9 9.2 %copy-start.5 = (bf16[8,64,128]{2,1,0:T(8,128)(2,1)}, bf16[8,64,128]{2,1,0:T(8,128)(2,1)S(1)}, u32[]{:S(2)}) copy-start(bf16[8,64,128]{2,1,0:T(8,128)(2,1)S(1)} %all-to-all-done.3) | copy-start | bytes 393220
  40.9 22.7 %all-to-all-start.1 = ((bf16[8,64,768]{2,1,0:T(8,128)(2,1)}), bf16[8,64,768]{2,1,0:T(8,128)(2,1)S(1)}, u32[]{:S(2)}, u32[]{:S(2)}) async-start(bf16[8,64,768]{2,1,0:T(8,128)(2,1)} %bitcast.4), calls=%async_computation.1 | async-start | bytes 1572864 | tf_op jit(solution)/shard_map/all_to_all | solution.py:112
  46.4 91.5 %all-gather.4.cloned.1.call-start = ((), (), s32[]{:S(2)}) async-start(), calls=%async_computation.8 | async-start | bytes 1769472 | tf_op jit(solution)/shard_map/all_gather | solution.py:18
  50.0 0.6 copy-start.7
  54.0 0.6 copy-start.3
  56.9 6.8 %copy-start.2 = (bf16[512,128]{1,0:T(8,128)(2,1)}, bf16[512,128]{1,0:T(8,128)(2,1)S(1)}, u32[]{:S(2)}) copy-start(bf16[512,128]{1,0:T(8,128)(2,1)S(1)} %scatter_custom_fusion.6) | copy-start | bytes 393220
  67.4 1.5 copy-start.4
  73.5 9.6 %all-to-all-start.2 = ((bf16[8,64,128]{2,1,0:T(8,128)(2,1)}), bf16[8,64,128]{2,1,0:T(8,128)(2,1)S(1)}, u32[]{:S(2)}, u32[]{:S(2)}) async-start(bf16[8,64,128]{2,1,0:T(8,128)(2,1)} %bitcast.7), calls=%async_computation.2 | async-start | bytes 262144 | tf_op jit(solution)/shard_map/all_to_all | solution.py:115
  83.1 6.3 %copy-start.6 = (bf16[8,64,128]{2,1,0:T(8,128)(2,1)}, bf16[8,64,128]{2,1,0:T(8,128)(2,1)S(1)}, u32[]{:S(2)}) copy-start(bf16[8,64,128]{2,1,0:T(8,128)(2,1)S(1)} %all-to-all-done.2) | copy-start | bytes 393220
  83.1 44.8 %all-to-all-start.5 = ((bf16[8,64,768]{2,1,0:T(8,128)(2,1)}), bf16[8,64,768]{2,1,0:T(8,128)(2,1)}, u32[]{:S(2)}, u32[]{:S(2)}) async-start(bf16[8,64,768]{2,1,0:T(8,128)(2,1)} %bitcast.70), calls=%async_computation.5 | async-start | bytes 1572864 | tf_op jit(solution)/shard_map/all_to_all | solution.py:113
  89.4 113.4 %reduce-scatter.2.cloned.1.call-start = ((), (), s32[]{:S(2)}) async-start(), calls=%async_computation.7 | async-start | bytes 1966080 | tf_op jit(solution)/shard_map/reduce_scatter | solution.py:196
  137.9 8.7 %copy-start.8 = (f32[12]{0:T(128)S(1)}, f32[12]{0:T(128)}, u32[]{:S(2)}) copy-start(f32[12]{0:T(128)} %param.19) | copy-start | bytes 148
  150.1 3.1 %copy-start.1 = (bf16[512,768]{1,0:T(8,128)(2,1)S(1)}, bf16[512,768]{1,0:T(8,128)(2,1)}, u32[]{:S(2)}) copy-start(bf16[512,768]{1,0:T(8,128)(2,1)} %scatter_custom_fusion.10) | copy-start | bytes 2359300
  153.2 15.9 %copy-start.9 = (f32[768]{0:T(1024)S(1)}, f32[768]{0:T(1024)}, u32[]{:S(2)}) copy-start(f32[768]{0:T(1024)} %param.20) | copy-start | bytes 9220
Sparse Core Ops, SparseCore 0:
  71.0 51.4 all-gather.3
  173.5 29.2 reduce-scatter.1
where the time goes:
time: 213 us; the launch traced here: 210 us
  blocking collectives  44.2 us (21%)
  local copies, waits for them, and re-layouts  42.2 us (20%)
  waiting for transfers between devices  35.5 us (17%)
  starting transfers between devices  33.5 us (16%)
  other arithmetic  21.3 us (10%)
  matrix products  17.8 us (8%)
  between operations  14.8 us (7%)
    all_gather x1, blocking collectives, prefix(): lax.all_gather(part.astype(kind), axis)  30.3 us
    reduce_scatter x1, waiting for transfers between devices, body(): lax.psum_scatter(jnp.dot(normed, out_weight, preferred_element_type=jnp.f...  29.5 us
    scatter x6, local copies, waits for them, and re-layouts, unpack_rows(): return blank.at[arrived].set(flattened, mode='drop')  16 us
    scatter x5, local copies, waits for them, and re-layouts, pack_rows(): blank.at[slot_index].set(values)  15.4 us
    psum x1, blocking collectives, body(): squares = lax.psum(jnp.sum(gated * gated, axis=1), 'head')  13.9 us
    select_n x8, other arithmetic, hop(): return jax.tree.map(lambda a, b: jnp.where(reached, a, b), new, before)  8.41 us
    all_to_all x1, starting transfers between devices, body(): lax.all_to_all(pack_rows(gate_in), 'seq', split_axis=0, concat_axis=0, ti...  6.29 us
    all_to_all x1, waiting for transfers between devices, body(): lax.all_to_all(pack_rows(features_in), 'seq', split_axis=0, concat_axis=0...  6.03 us
  transfers between devices with their start and end apart: 8, of which 2 were waited for; matrix products, arithmetic and copies ran while one was open for 22% of the time, Pallas kernels for 0%

commit v1 on v0

v1 whole, which is shorter than its diff:
```python
import functools

import jax
import jax.numpy as jnp
from jax import lax
from jax.experimental import pallas as pl
from jax.experimental.pallas import tpu as pltpu
from jax.sharding import PartitionSpec as P

ATTENTION_LANES = 48
HEAD_DIM = 64
NORM_EPS = 1e-05
LANES = 128
F32 = jnp.float32
BF16 = jnp.bfloat16
MESH = pl.DeviceIdType.MESH


def iota(shape, axis):
    return lax.broadcasted_iota(jnp.int32, shape, axis)


def dot(a, b):
    return jnp.dot(a, b, preferred_element_type=F32)


def dot_nt(a, b):
    return lax.dot_general(a, b, (((1,), (1,)), ((), ())), preferred_element_type=F32)


def layer_kernel(
    n,
    steps,
    heads,
    docs,
    target_ref,
    doc_ref,
    skip_ref,
    x_ref,
    z_ref,
    b_ref,
    c_ref,
    small_ref,
    gain_ref,
    w_ref,
    out_ref,
    send_aux,
    send_x,
    send_z,
    recv_aux,
    recv_x,
    recv_z,
    state_send,
    state_recv,
    xs_ref,
    xw_ref,
    zs_ref,
    cs_ref,
    gm_ref,
    mixed_ref,
    gs_ref,
    sq_ref,
    sq_recv,
    a_send,
    a_recv,
    y_send,
    y_recv,
    out_sem,
    in_sem,
    state_out_sem,
    state_in_sem,
    head_out_sem,
    head_in_sem,
):
    tok, wide = x_ref.shape
    cap = tok // n
    state = b_ref.shape[1]
    pairs = wide // LANES
    half = tok // 2
    own = tok // 4
    me = lax.axis_index("seq")
    hd = lax.axis_index("head")
    core, side = hd % 2, hd // 2
    core_peer = side * 2 + (1 - core)
    side_peer = (1 - side) * 2 + core

    barrier = pltpu.get_barrier_semaphore()

    def greet(k, carry):
        pl.semaphore_signal(
            barrier, inc=1, device_id={"seq": (me + k) % n}, device_id_type=MESH
        )
        return carry

    lax.fori_loop(1, n, greet, 0)
    for k in range(1, 4):
        pl.semaphore_signal(
            barrier, inc=1, device_id={"head": (hd + k) % 4}, device_id_type=MESH
        )

    target = target_ref[...]
    owner = target // tok
    place = target - owner * tok
    far = (owner - me + n) % n
    groups = max(n, 16)
    hits = (iota((groups, tok), 0) == far).astype(F32)
    before = (iota((tok, tok), 0) < iota((tok, tok), 1)).astype(F32).astype(BF16)
    rank = jnp.sum(dot(hits.astype(BF16), before) * hits, axis=0, keepdims=True)
    slot = far * cap + rank.astype(jnp.int32)
    perm = (iota((tok, tok), 0) == slot).astype(F32).astype(BF16)
    high = place // 16
    row = iota((LANES, tok), 0)
    small_t = jnp.where(
        row == heads,
        high.astype(F32),
        jnp.where(row == heads + 1, (place - high * 16).astype(F32), small_ref[...].astype(F32)),
    ).astype(BF16)

    def copy_of(which, send, recv, k):
        return pltpu.make_async_remote_copy(
            src_ref=send.at[k],
            dst_ref=recv.at[k],
            send_sem=out_sem.at[which, k],
            recv_sem=in_sem.at[which, k],
            device_id={"seq": (me + k) % n},
            device_id_type=MESH,
        )

    def start_all(which, send, recv, first, last):
        def go(k, carry):
            copy_of(which, send, recv, k).start()
            return carry

        lax.fori_loop(first, last, go, 0)

    def wait_in(which, send, recv):
        def go(k, carry):
            copy_of(which, send, recv, k).wait_recv()
            return carry

        lax.fori_loop(1, n, go, 0)

    def wait_out(which, send, recv):
        def go(k, carry):
            copy_of(which, send, recv, k).wait_send()
            return carry

        lax.fori_loop(1, n, go, 0)

    def by_slot(values):
        return values.reshape(values.shape[0] // cap, cap, values.shape[1]).astype(BF16)

    def packed_rows(ref):
        if cap % 16 == 0:
            return ref[...].reshape(tok, ref.shape[2])
        return ref[...].astype(F32).reshape(tok, ref.shape[2]).astype(BF16)

    send_aux[:, :, 0:state] = by_slot(dot(perm, b_ref[...]))
    send_aux[:, :, state : 2 * state] = by_slot(dot(perm, c_ref[...]))
    send_aux[:, :, 2 * state :] = by_slot(dot_nt(perm, small_t))
    pl.semaphore_wait(barrier, n - 1 + 3)
    start_all(0, send_aux, recv_aux, 1, n)
    recv_aux[0] = send_aux[0]
    for part in range(2):
        lo, hi = part * n // 2, (part + 1) * n // 2
        send_x[lo:hi] = by_slot(dot(perm[lo * cap : hi * cap], x_ref[...]))
        start_all(1, send_x, recv_x, max(lo, 1), hi)
    recv_x[0] = send_x[0]
    send_z[...] = by_slot(dot(perm, z_ref[...]))
    start_all(2, send_z, recv_z, 1, n)
    recv_z[0] = send_z[0]

    first_place = me * tok
    col = iota((tok, 1), 0)
    line = iota((1, tok), 1)
    doc_col = jnp.zeros((tok, 1), jnp.int32)
    doc_line = jnp.zeros((1, tok), jnp.int32)
    doc_last = jnp.int32(0)
    doc_before = jnp.int32(0)
    start = jnp.int32(0)
    for k in range(docs):
        doc_col += jnp.where(col + first_place >= start, 1, 0)
        doc_line += jnp.where(line + first_place >= start, 1, 0)
        doc_last += jnp.where(first_place + tok - 1 >= start, 1, 0)
        doc_before += jnp.where(first_place - 1 >= start, 1, 0)
        start = start + doc_ref[k]
    low = iota((tok, tok), 0) >= iota((tok, tok), 1)
    lane = iota((1, LANES), 1)
    left = lane < HEAD_DIM

    wait_in(0, send_aux, recv_aux)
    aux = packed_rows(recv_aux)
    small_back = aux[:, 2 * state :].astype(F32).T
    places = small_back[heads : heads + 1] * 16.0 + small_back[heads + 1 : heads + 2]
    unperm = (iota((tok, tok), 0) == places.astype(jnp.int32)).astype(F32).astype(BF16)
    aux = dot(unperm, aux)
    b_t = aux[:, 0:state].T.astype(BF16)
    cs_ref[...] = aux[:, state : 2 * state].astype(BF16)
    decays = jnp.where(lane < heads, aux[:, 2 * state :], 0.0).astype(BF16)
    running = dot(low.astype(F32).astype(BF16), decays)
    running_t = running.T
    closing = running[tok - 1 : tok]
    weight = jnp.exp(closing - running) * jnp.where(doc_col == doc_last, 1.0, 0.0)
    entry = jnp.exp(running) * jnp.where(doc_col == doc_before, 1.0, 0.0)
    through = jnp.exp(closing) * jnp.where(doc_last == doc_before, 1.0, 0.0)
    allowed = low & (doc_col == doc_line)
    gm_ref[...] = jnp.where(allowed, dot(cs_ref[...], b_t), 0.0)

    def spread(values, j):
        return jnp.where(left, values[:, 2 * j : 2 * j + 1], values[:, 2 * j + 1 : 2 * j + 2])

    wait_in(1, send_x, recv_x)
    xs_ref[...] = dot(unperm, packed_rows(recv_x)).astype(BF16)
    for j in range(pairs):
        cols = slice(j * LANES, (j + 1) * LANES)
        xw_ref[:, cols] = (xs_ref[:, cols].astype(F32) * spread(weight, j)).astype(BF16)
    held = dot(b_t, xw_ref[...])
    kept = jnp.concatenate([spread(through, j) for j in range(pairs)], axis=1)

    def state_copy(step):
        gap = 1 if step == 0 else 2 ** (step - 1)
        copy = pltpu.make_async_remote_copy(
            src_ref=state_send.at[step],
            dst_ref=state_recv.at[step],
            send_sem=state_out_sem.at[step],
            recv_sem=state_in_sem.at[step],
            device_id={"seq": (me + gap) % n},
            device_id_type=MESH,
        )
        return copy, gap

    def state_start(step, held, kept):
        state_send[step, 0:state] = held.astype(BF16)
        upper = kept.astype(BF16).astype(F32)
        rows = iota((16, wide), 0)
        state_send[step, state:] = jnp.where(
            rows == 0, upper, jnp.where(rows == 1, kept - upper, 0.0)
        ).astype(BF16)
        copy, gap = state_copy(step)

        @pl.when(me + gap < n)
        def _():
            copy.start()

    def state_finish(step, held, kept):
        copy, gap = state_copy(step)

        @pl.when(me >= gap)
        def _():
            copy.wait_recv()

        @pl.when(me < gap)
        def _():
            state_recv[step] = jnp.zeros(state_recv.shape[1:], BF16)

        came = state_recv[step, 0:state].astype(F32)
        tail = state_recv[step, state:].astype(F32)
        came_kept = tail[0:1] + tail[1:2]
        if step == 0:
            return came, came_kept
        return held + kept * came, kept * came_kept

    def inner(j):
        cols = slice(j * LANES, (j + 1) * LANES)
        skip = jnp.where(left, skip_ref[2 * j], skip_ref[2 * j + 1])
        for t0 in range(0, tok, half):
            rows = slice(t0, t0 + half)
            upto = t0 + half
            keys = xs_ref[0:upto, cols]
            sums = []
            for h in (2 * j, 2 * j + 1):
                gaps = jnp.minimum(
                    running[rows, h : h + 1] - running_t[h : h + 1, 0:upto], 0.0
                )
                scores = (gm_ref[rows, 0:upto] * jnp.exp(gaps)).astype(BF16)
                sums.append(dot(scores, keys))
            mixed_ref[rows, cols] = (
                jnp.where(left, sums[0], sums[1]) + skip * xs_ref[rows, cols].astype(F32)
            )

    state_start(0, held, kept)
    done = 0
    for step in range(steps):
        until = pairs * (step + 1) // steps
        for j in range(done, until):
            inner(j)
        done = until
        if step == steps - 1:
            wait_in(2, send_z, recv_z)
            zs_ref[...] = dot(unperm, packed_rows(recv_z)).astype(BF16)
        held, kept = state_finish(step, held, kept)
        if step + 1 < steps:
            state_start(step + 1, held, kept)
    entry_state = held.astype(BF16)
    mixed_ref[...] += dot(cs_ref[...], entry_state) * jnp.concatenate(
        [spread(entry, j) for j in range(pairs)], axis=1
    )

    def gate_half(where):
        rows = pl.ds(pl.multiple_of(where * half, half), half)
        gate = zs_ref[rows, :].astype(F32)
        gated = mixed_ref[rows, :] * (gate / (1.0 + jnp.exp(-gate)))
        gs_ref[rows, :] = (gated * gain_ref[...]).astype(BF16)
        squares = jnp.sum(gated * gated, axis=1, keepdims=True)
        squares = jnp.broadcast_to(squares, (half, LANES)).T[0:8]
        for i in range(2):
            sq_ref[pl.ds(2 * where + i, 1)] = squares[None, :, i * own : (i + 1) * own]

    def partial(where_side, where_core):
        at = (where_side * 2 + where_core) * own
        return dot(gs_ref[pl.ds(pl.multiple_of(at, own), own), :], w_ref[...])

    def head_copy(which, src, dst, peer):
        return pltpu.make_async_remote_copy(
            src_ref=src,
            dst_ref=dst,
            send_sem=head_out_sem.at[which],
            recv_sem=head_in_sem.at[which],
            device_id={"head": peer},
            device_id_type=MESH,
        )

    copies = [head_copy(i, a_send.at[i], a_recv.at[i], core_peer) for i in range(2)]
    across = head_copy(2, y_send, y_recv, side_peer)
    gate_half(1 - side)
    a_send[0] = partial(1 - side, 1 - core).astype(BF16)
    copies[0].start()
    passing = partial(1 - side, core)
    copies[0].wait_recv()
    y_send[...] = (passing + a_recv[0].astype(F32)).astype(BF16)
    across.start()
    gate_half(side)
    sq_copies = [
        head_copy(2 + k, sq_ref.at[(hd + k) % 4], sq_recv.at[k], (hd + k) % 4) for k in range(1, 4)
    ]
    for copy in sq_copies:
        copy.start()
    a_send[1] = partial(side, 1 - core).astype(BF16)
    copies[1].start()
    total = partial(side, core)
    for copy in sq_copies:
        copy.wait_recv()
    squares = sq_ref[pl.ds(hd, 1)][0] + sq_recv[1] + sq_recv[2] + sq_recv[3]
    scale = lax.rsqrt(squares / (ATTENTION_LANES * HEAD_DIM) + NORM_EPS)
    scale = jnp.broadcast_to(scale[0:1], (LANES, own)).T[:, 0:1]
    copies[1].wait_recv()
    total = total + a_recv[1].astype(F32)
    across.wait_recv()
    out_ref[...] = ((total + y_recv[...].astype(F32)) * scale).astype(BF16)

    wait_out(0, send_aux, recv_aux)
    wait_out(1, send_x, recv_x)
    wait_out(2, send_z, recv_z)
    for step in range(steps):
        copy, gap = state_copy(step)

        @pl.when(me + gap < n)
        def _():
            copy.wait_send()

    for copy in copies + [across] + sq_copies:
        copy.wait_send()


def body(
    features_in,
    gate_in,
    b_input,
    c_input,
    log_decay,
    row_target,
    doc_lengths,
    skip_gain,
    norm_gain,
    out_weight,
):
    tok, wide = features_in.shape
    heads = log_decay.shape[1]
    state = b_input.shape[1]
    model = out_weight.shape[1]
    n = lax.axis_size("seq")
    cap = tok // n
    aux = 2 * state + LANES
    steps, reach = 1, 1
    while reach < n // 2:
        steps, reach = steps + 1, reach * 2
    small = jnp.pad(log_decay.T, ((0, LANES - heads), (0, 0)))
    vmem = pl.BlockSpec(memory_space=pltpu.VMEM)
    smem = pl.BlockSpec(memory_space=pltpu.SMEM)
    own = tok // 4
    kernel = functools.partial(layer_kernel, n, steps, heads, doc_lengths.shape[0])
    return pl.pallas_call(
        kernel,
        out_shape=jax.ShapeDtypeStruct((own, model), BF16),
        in_specs=[vmem, smem, smem] + [vmem] * 7,
        out_specs=vmem,
        scratch_shapes=[
            pltpu.VMEM((n, cap, aux), BF16),
            pltpu.VMEM((n, cap, wide), BF16),
            pltpu.VMEM((n, cap, wide), BF16),
            pltpu.VMEM((n, cap, aux), BF16),
            pltpu.VMEM((n, cap, wide), BF16),
            pltpu.VMEM((n, cap, wide), BF16),
            pltpu.VMEM((steps, state + 16, wide), BF16),
            pltpu.VMEM((steps, state + 16, wide), BF16),
            pltpu.VMEM((tok, wide), BF16),
            pltpu.VMEM((tok, wide), BF16),
            pltpu.VMEM((tok, wide), BF16),
            pltpu.VMEM((tok, state), BF16),
            pltpu.VMEM((tok, tok), F32),
            pltpu.VMEM((tok, wide), F32),
            pltpu.VMEM((tok, wide), BF16),
            pltpu.VMEM((4, 8, own), F32),
            pltpu.VMEM((4, 8, own), F32),
            pltpu.VMEM((2, own, model), BF16),
            pltpu.VMEM((2, own, model), BF16),
            pltpu.VMEM((own, model), BF16),
            pltpu.VMEM((own, model), BF16),
            pltpu.SemaphoreType.DMA((3, n)),
            pltpu.SemaphoreType.DMA((3, n)),
            pltpu.SemaphoreType.DMA((steps,)),
            pltpu.SemaphoreType.DMA((steps,)),
            pltpu.SemaphoreType.DMA((6,)),
            pltpu.SemaphoreType.DMA((6,)),
        ],
        compiler_params=pltpu.CompilerParams(
            collective_id=0, has_side_effects=True, vmem_limit_bytes=52 * 1024 * 1024
        ),
        name="layer",
    )(
        row_target.reshape(1, tok),
        doc_lengths,
        skip_gain,
        features_in,
        gate_in,
        b_input,
        c_input,
        small,
        norm_gain.reshape(1, wide),
        out_weight,
    )


def solution(mesh):
    in_specs = (
        P("seq", "head"),
        P("seq", "head"),
        P("seq", None),
        P("seq", None),
        P("seq", "head"),
        P("seq"),
        P(),
        P("head"),
        P("head"),
        P("head", None),
    )
    out_specs = P(("seq", "head"), None)
    return jax.shard_map(body, mesh=mesh, in_specs=in_specs, out_specs=out_specs, check_vma=False)
```

time: 213 us -> 86.8 us (0.41); the launches traced: 210 us -> 86.2 us
  Pallas kernels: 0 us -> 79.1 us
  blocking collectives: 44.2 us -> 0 us
  waiting for transfers between devices: 35.5 us -> 0 us
  local copies, waits for them, and re-layouts: 42.2 us -> 7.09 us
  starting transfers between devices: 33.5 us -> 0 us
  other arithmetic: 21.3 us -> 0 us
  matrix products: 17.8 us -> 0 us
  between operations: 14.8 us -> 0.03 us
    pallas_call x0 -> x1, Pallas kernels: none -> 79.1 us  [body(): pl.pallas_call(kernel, out_shape=jax.ShapeDtypeStruct((own, model), BF16)...]
    scatter x12 -> x0, local copies, waits for them, and re-layouts: 33.9 us -> none  [the longest x6 16 us: unpack_rows(): return blank.at[arrived].set(flattened, mode='drop')]
    all_to_all x6 -> x0, starting transfers between devices: 33.5 us -> none  [the longest x1 6.29 us: body(): lax.all_to_all(pack_rows(gate_in), 'seq', split_axis=0, concat_axis=0, ti...]
    all_gather x1 -> x0, blocking collectives: 30.3 us -> none  [prefix(): lax.all_gather(part.astype(kind), axis)]
    reduce_scatter x1 -> x0, waiting for transfers between devices: 29.5 us -> none  [body(): lax.psum_scatter(jnp.dot(normed, out_weight, preferred_element_type=jnp.f...]
    dot_general x5 -> x0, matrix products: 17.8 us -> none  [the longest x1 5.82 us: inner_terms(): jnp.einsum('hts,shp->thp', affinity_logits, by_head, preferred_element_ty...]
    psum x1 -> x0, blocking collectives: 13.9 us -> none  [body(): squares = lax.psum(jnp.sum(gated * gated, axis=1), 'head')]
    select_n x10 -> x0, other arithmetic: 8.43 us -> none  [the longest x8 8.41 us: hop(): return jax.tree.map(lambda a, b: jnp.where(reached, a, b), new, before)]
  transfers between devices with their start and end apart: 8 -> 0, of which waited for: 2 -> 0; matrix products, arithmetic and copies ran while one was open for 22% -> 0% of each run, Pallas kernels for 0% -> 0%
where the time goes in v1:
time: 86.8 us; the launch traced here: 86.2 us
  Pallas kernels  79.1 us (91%)
  local copies, waits for them, and re-layouts  7.09 us (8%)
    pallas_call x1, Pallas kernels, body(): pl.pallas_call(kernel, out_shape=jax.ShapeDtypeStruct((own, model), BF16)...  79.1 us
    unnamed x13, local copies, waits for them, and re-layouts  5.67 us

profile of v1, /device:TPU:27, one launch (start us, length us, event | category | flops | bytes accessed | tf_op | source)
XLA Modules:
  0.0 86.2 jit_solution(12075808363928925017)
XLA Ops:
  0.0 0.7 reshape.7.gain_ref
  0.7 0.7 pad.4.small_ref
  1.4 0.0 copy-start
  1.4 1.1 %copy-done = bf16[512,768]{1,0:T(8,128)(2,1)S(1)} copy-done((bf16[512,768]{1,0:T(8,128)(2,1)S(1)}, bf16[512,768]{1,0:T(8,128)(2,1)}, u32[]{:S(2)}) %copy-start) | copy-done | bytes 786456
  2.6 0.0 copy-start.1
  2.6 0.9 %copy-done.1 = bf16[512,128]{1,0:T(8,128)(2,1)S(1)} copy-done((bf16[512,128]{1,0:T(8,128)(2,1)S(1)}, bf16[512,128]{1,0:T(8,128)(2,1)}, u32[]{:S(2)}) %copy-start.1) | copy-done | bytes 131096
  3.5 0.0 copy-start.2
  3.5 0.9 %copy-done.2 = bf16[512,128]{1,0:T(8,128)(2,1)S(1)} copy-done((bf16[512,128]{1,0:T(8,128)(2,1)S(1)}, bf16[512,128]{1,0:T(8,128)(2,1)}, u32[]{:S(2)}) %copy-start.2) | copy-done | bytes 131096
  4.4 0.0 copy-start.3
  4.4 0.7 copy-done.3
  5.0 0.0 copy-start.4
  5.1 0.7 copy-done.4
  5.7 0.0 copy-start.5
  5.7 0.7 copy-done.5
  6.4 79.1 %layer.1 = bf16[128,1536]{1,0:T(8,128)(2,1)S(1)} custom-call(s32[1,512]{1,0:T(1,128)S(1)} %bitcast.2, s32[4]{0:T(128)S(1)} %copy-done.4, f32[12]{0:T(128)S(1)} %copy-done.5, bf16[512,768]{1,0:T(8,128)(2,1)S(1)} %copy-done, bf16[512,768]{1,0:T(8,128)(2,1)} %z_ref.1, bf16[512,128]{1,0:T(8,128)(2,1)S(1)} %copy-done.1, bf16[512,128]{1,0:T(8,128)(2,1)S(1)} %copy-done.2, ...), custom_call_target="tpu_custom_call" | custom-call | tf_op jit(solution)/shard_map/layer/pallas_call | solution.py:392
  85.5 0.7 copy.12
Async XLA Ops:
  1.4 1.1 %copy-start = (bf16[512,768]{1,0:T(8,128)(2,1)S(1)}, bf16[512,768]{1,0:T(8,128)(2,1)}, u32[]{:S(2)}) copy-start(bf16[512,768]{1,0:T(8,128)(2,1)} %x_ref.1) | copy-start | bytes 2359300
  2.6 0.9 %copy-start.1 = (bf16[512,128]{1,0:T(8,128)(2,1)S(1)}, bf16[512,128]{1,0:T(8,128)(2,1)}, u32[]{:S(2)}) copy-start(bf16[512,128]{1,0:T(8,128)(2,1)} %b_ref.1) | copy-start | bytes 393220
  3.5 0.9 %copy-start.2 = (bf16[512,128]{1,0:T(8,128)(2,1)S(1)}, bf16[512,128]{1,0:T(8,128)(2,1)}, u32[]{:S(2)}) copy-start(bf16[512,128]{1,0:T(8,128)(2,1)} %c_ref.1) | copy-start | bytes 393220
  4.4 0.7 copy-start.3
  5.0 0.7 copy-start.4
  5.7 0.7 copy-start.5

commit v2 on v1

--- a/solution.py
+++ b/solution.py
@@ -30,28 +30,44 @@
 
 def layer_kernel(
     n,
-    steps,
+    gaps,
     heads,
     docs,
     target_ref,
     doc_ref,
     skip_ref,
+    x_hbm,
+    z_hbm,
+    b_hbm,
+    c_hbm,
+    small_ref,
+    gain_ref,
+    w_hbm,
+    out_ref,
     x_ref,
     z_ref,
     b_ref,
     c_ref,
-    small_ref,
-    gain_ref,
     w_ref,
-    out_ref,
+    small_f,
+    load_sem,
+    send_bc,
+    recv_bc,
+    bc_out_sem,
+    bc_in_sem,
+    share_sem,
     send_aux,
     send_x,
     send_z,
     recv_aux,
     recv_x,
     recv_z,
+    pair_send,
+    pair_recv,
     state_send,
     state_recv,
+    last_send,
+    last_recv,
     xs_ref,
     xw_ref,
     zs_ref,
@@ -84,6 +100,23 @@
     core_peer = side * 2 + (1 - core)
     side_peer = (1 - side) * 2 + core
 
+    column = me % 2
+    pair_peer = me + 1 - 2 * column
+    loads = [
+        pltpu.make_async_copy(src, dst, load_sem.at[i])
+        for i, (src, dst) in enumerate(
+            (
+                (b_hbm, b_ref),
+                (c_hbm, c_ref),
+                (x_hbm, x_ref),
+                (z_hbm, z_ref),
+                (w_hbm, w_ref),
+            )
+        )
+    ]
+    for load in loads:
+        load.start()
+
     barrier = pltpu.get_barrier_semaphore()
 
     def greet(k, carry):
@@ -109,12 +142,11 @@
     slot = far * cap + rank.astype(jnp.int32)
     perm = (iota((tok, tok), 0) == slot).astype(F32).astype(BF16)
     high = place // 16
-    row = iota((LANES, tok), 0)
-    small_t = jnp.where(
-        row == heads,
-        high.astype(F32),
-        jnp.where(row == heads + 1, (place - high * 16).astype(F32), small_ref[...].astype(F32)),
-    ).astype(BF16)
+    small_f[...] = jnp.zeros_like(small_f)
+    small_f[0:heads] = small_ref[...].astype(F32)
+    small_f[heads : heads + 1] = high.astype(F32)
+    small_f[heads + 1 : heads + 2] = (place - high * 16).astype(F32)
+    small_t = small_f[...].astype(BF16)
 
     def copy_of(which, send, recv, k):
         return pltpu.make_async_remote_copy(
@@ -155,17 +187,54 @@
             return ref[...].reshape(tok, ref.shape[2])
         return ref[...].astype(F32).reshape(tok, ref.shape[2]).astype(BF16)
 
-    send_aux[:, :, 0:state] = by_slot(dot(perm, b_ref[...]))
-    send_aux[:, :, state : 2 * state] = by_slot(dot(perm, c_ref[...]))
-    send_aux[:, :, 2 * state :] = by_slot(dot_nt(perm, small_t))
+    def bc_copy(k):
+        return pltpu.make_async_remote_copy(
+            src_ref=send_bc.at[k],
+            dst_ref=recv_bc.at[k],
+            send_sem=bc_out_sem.at[k],
+            recv_sem=bc_in_sem.at[k],
+            device_id={"seq": (me + k) % n},
+            device_id_type=MESH,
+        )
+
+    def bc_share(i, p):
+        k = hd + 4 * i
+        return pltpu.make_async_remote_copy(
+            src_ref=recv_bc.at[k],
+            dst_ref=recv_bc.at[k],
+            send_sem=share_sem.at[i, p],
+            recv_sem=bc_in_sem.at[k],
+            device_id={"head": (hd + p) % 4},
+            device_id_type=MESH,
+        )
+
+    def mine(act):
+        def go(i, carry):
+            @pl.when(hd + 4 * i >= 1)
+            def _():
+                act(i, hd + 4 * i)
+
+            return carry
+
+        lax.fori_loop(0, n // 4, go, 0)
+
+    loads[0].wait()
+    loads[1].wait()
+    send_bc[:, :, 0:state] = by_slot(dot(perm, b_ref[...]))
+    send_bc[:, :, state:] = by_slot(dot(perm, c_ref[...]))
+    send_aux[...] = by_slot(dot_nt(perm, small_t))
     pl.semaphore_wait(barrier, n - 1 + 3)
+    mine(lambda i, k: bc_copy(k).start())
     start_all(0, send_aux, recv_aux, 1, n)
     recv_aux[0] = send_aux[0]
+    recv_bc[0] = send_bc[0]
+    loads[2].wait()
     for part in range(2):
         lo, hi = part * n // 2, (part + 1) * n // 2
         send_x[lo:hi] = by_slot(dot(perm[lo * cap : hi * cap], x_ref[...]))
         start_all(1, send_x, recv_x, max(lo, 1), hi)
     recv_x[0] = send_x[0]
+    loads[3].wait()
     send_z[...] = by_slot(dot(perm, z_ref[...]))
     start_all(2, send_z, recv_z, 1, n)
     recv_z[0] = send_z[0]
@@ -188,15 +257,31 @@
     lane = iota((1, LANES), 1)
     left = lane < HEAD_DIM
 
+    def share(i, k):
+        bc_copy(k).wait_recv()
+        for p in range(1, 4):
+            bc_share(i, p).start()
+
+    mine(share)
     wait_in(0, send_aux, recv_aux)
     aux = packed_rows(recv_aux)
-    small_back = aux[:, 2 * state :].astype(F32).T
+    small_back = aux.astype(F32).T
     places = small_back[heads : heads + 1] * 16.0 + small_back[heads + 1 : heads + 2]
     unperm = (iota((tok, tok), 0) == places.astype(jnp.int32)).astype(F32).astype(BF16)
     aux = dot(unperm, aux)
-    b_t = aux[:, 0:state].T.astype(BF16)
-    cs_ref[...] = aux[:, state : 2 * state].astype(BF16)
-    decays = jnp.where(lane < heads, aux[:, 2 * state :], 0.0).astype(BF16)
+
+    def shared(k, carry):
+        @pl.when(k % 4 != hd)
+        def _():
+            bc_copy(k).wait_recv()
+
+        return carry
+
+    lax.fori_loop(1, n, shared, 0)
+    both = dot(unperm, packed_rows(recv_bc))
+    b_t = both[:, 0:state].T.astype(BF16)
+    cs_ref[...] = both[:, state:].astype(BF16)
+    decays = jnp.where(lane < heads, aux, 0.0).astype(BF16)
     running = dot(low.astype(F32).astype(BF16), decays)
     running_t = running.T
     closing = running[tok - 1 : tok]
@@ -217,48 +302,55 @@
     held = dot(b_t, xw_ref[...])
     kept = jnp.concatenate([spread(through, j) for j in range(pairs)], axis=1)
 
+    def fill(ref, held, kept):
+        ref[0:state] = held.astype(BF16)
+        upper = kept.astype(BF16).astype(F32)
+        rows = iota((16, kept.shape[1]), 0)
+        ref[state:] = jnp.where(
+            rows == 0, upper, jnp.where(rows == 1, kept - upper, 0.0)
+        ).astype(BF16)
+
+    def read(ref):
+        tail = ref[state:].astype(F32)
+        return ref[0:state].astype(F32), tail[0:1] + tail[1:2]
+
+    def pair_copy(which, src, dst):
+        return pltpu.make_async_remote_copy(
+            src_ref=src,
+            dst_ref=dst,
+            send_sem=state_out_sem.at[which],
+            recv_sem=state_in_sem.at[which],
+            device_id={"seq": pair_peer},
+            device_id_type=MESH,
+        )
+
     def state_copy(step):
-        gap = 1 if step == 0 else 2 ** (step - 1)
-        copy = pltpu.make_async_remote_copy(
+        return pltpu.make_async_remote_copy(
             src_ref=state_send.at[step],
             dst_ref=state_recv.at[step],
-            send_sem=state_out_sem.at[step],
-            recv_sem=state_in_sem.at[step],
-            device_id={"seq": (me + gap) % n},
+            send_sem=state_out_sem.at[2 + step],
+            recv_sem=state_in_sem.at[2 + step],
+            device_id={"seq": (me + 2 * gaps[step]) % n},
             device_id_type=MESH,
         )
-        return copy, gap
 
     def state_start(step, held, kept):
-        state_send[step, 0:state] = held.astype(BF16)
-        upper = kept.astype(BF16).astype(F32)
-        rows = iota((16, wide), 0)
-        state_send[step, state:] = jnp.where(
-            rows == 0, upper, jnp.where(rows == 1, kept - upper, 0.0)
-        ).astype(BF16)
-        copy, gap = state_copy(step)
-
-        @pl.when(me + gap < n)
+        fill(state_send.at[step], held, kept)
+
+        @pl.when(me + 2 * gaps[step] < n)
         def _():
-            copy.start()
-
-    def state_finish(step, held, kept):
-        copy, gap = state_copy(step)
-
-        @pl.when(me >= gap)
+            state_copy(step).start()
+
+    def state_finish(step):
+        @pl.when(me >= 2 * gaps[step])
         def _():
-            copy.wait_recv()
-
-        @pl.when(me < gap)
+            state_copy(step).wait_recv()
+
+        @pl.when(me < 2 * gaps[step])
         def _():
             state_recv[step] = jnp.zeros(state_recv.shape[1:], BF16)
 
-        came = state_recv[step, 0:state].astype(F32)
-        tail = state_recv[step, state:].astype(F32)
-        came_kept = tail[0:1] + tail[1:2]
-        if step == 0:
-            return came, came_kept
-        return held + kept * came, kept * came_kept
+        return read(state_recv.at[step])
 
     def inner(j):
         cols = slice(j * LANES, (j + 1) * LANES)
@@ -278,19 +370,49 @@
                 jnp.where(left, sums[0], sums[1]) + skip * xs_ref[rows, cols].astype(F32)
             )
 
-    state_start(0, held, kept)
-    done = 0
-    for step in range(steps):
-        until = pairs * (step + 1) // steps
-        for j in range(done, until):
+    stages = len(gaps) + 2
+
+    def inner_of(stage):
+        for j in range(pairs * stage // stages, pairs * (stage + 1) // stages):
             inner(j)
-        done = until
-        if step == steps - 1:
-            wait_in(2, send_z, recv_z)
-            zs_ref[...] = dot(unperm, packed_rows(recv_z)).astype(BF16)
-        held, kept = state_finish(step, held, kept)
-        if step + 1 < steps:
-            state_start(step + 1, held, kept)
+
+    first_copy = pair_copy(0, pair_send, pair_recv)
+    last_copy = pair_copy(1, last_send, last_recv)
+    fill(pair_send, held, kept)
+    first_copy.start()
+    inner_of(0)
+    first_copy.wait_recv()
+    part = wide // 2
+    other, other_kept = read(pair_recv)
+
+    def ordered(own_one, other_one):
+        early = jnp.where(column == 0, own_one, other_one)
+        late = jnp.where(column == 0, other_one, own_one)
+        return early, late
+
+    def my_half(values):
+        return jnp.where(column == 0, values[:, 0:part], values[:, part:])
+
+    early, late = ordered(my_half(held), my_half(other))
+    early_kept, late_kept = ordered(my_half(kept), my_half(other_kept))
+    sent, sent_kept = late + late_kept * early, late_kept * early_kept
+    for step in range(len(gaps)):
+        state_start(step, sent, sent_kept)
+        inner_of(1 + step)
+        came, came_kept = state_finish(step)
+        if step > 0:
+            came, came_kept = sent + sent_kept * came, sent_kept * came_kept
+        sent, sent_kept = came, came_kept
+    last_send[...] = sent.astype(BF16)
+    last_copy.start()
+    inner_of(stages - 1)
+    wait_in(2, send_z, recv_z)
+    zs_ref[...] = dot(unperm, packed_rows(recv_z)).astype(BF16)
+    last_copy.wait_recv()
+    early, late = ordered(last_send[...].astype(F32), last_recv[...].astype(F32))
+    held = jnp.concatenate([early, late], axis=1)
+    other, other_kept = read(pair_recv)
+    held = jnp.where(column == 0, held, other + other_kept * held)
     entry_state = held.astype(BF16)
     mixed_ref[...] += dot(cs_ref[...], entry_state) * jnp.concatenate(
         [spread(entry, j) for j in range(pairs)], axis=1
@@ -300,7 +422,7 @@
         rows = pl.ds(pl.multiple_of(where * half, half), half)
         gate = zs_ref[rows, :].astype(F32)
         gated = mixed_ref[rows, :] * (gate / (1.0 + jnp.exp(-gate)))
-        gs_ref[rows, :] = (gated * gain_ref[...]).astype(BF16)
+        gs_ref[rows, :] = (gated * gain_ref[...].reshape(1, wide)).astype(BF16)
         squares = jnp.sum(gated * gated, axis=1, keepdims=True)
         squares = jnp.broadcast_to(squares, (half, LANES)).T[0:8]
         for i in range(2):
@@ -320,6 +442,7 @@
             device_id_type=MESH,
         )
 
+    loads[4].wait()
     copies = [head_copy(i, a_send.at[i], a_recv.at[i], core_peer) for i in range(2)]
     across = head_copy(2, y_send, y_recv, side_peer)
     gate_half(1 - side)
@@ -351,12 +474,20 @@
     wait_out(0, send_aux, recv_aux)
     wait_out(1, send_x, recv_x)
     wait_out(2, send_z, recv_z)
-    for step in range(steps):
-        copy, gap = state_copy(step)
-
-        @pl.when(me + gap < n)
+    mine(lambda i, k: bc_copy(k).wait_send())
+
+    def shared_out(i, k):
+        for p in range(1, 4):
+            bc_share(i, p).wait_send()
+
+    mine(shared_out)
+    first_copy.wait_send()
+    last_copy.wait_send()
+    for step in range(len(gaps)):
+
+        @pl.when(me + 2 * gaps[step] < n)
         def _():
-            copy.wait_send()
+            state_copy(step).wait_send()
 
     for copy in copies + [across] + sq_copies:
         copy.wait_send()
@@ -380,29 +511,46 @@
     model = out_weight.shape[1]
     n = lax.axis_size("seq")
     cap = tok // n
-    aux = 2 * state + LANES
-    steps, reach = 1, 1
-    while reach < n // 2:
-        steps, reach = steps + 1, reach * 2
-    small = jnp.pad(log_decay.T, ((0, LANES - heads), (0, 0)))
+    aux = LANES
+    gaps, reach = [1], 1
+    while reach < n // 4:
+        gaps, reach = gaps + [reach], reach * 2
+    steps = len(gaps)
     vmem = pl.BlockSpec(memory_space=pltpu.VMEM)
     smem = pl.BlockSpec(memory_space=pltpu.SMEM)
+    hbm = pl.BlockSpec(memory_space=pltpu.HBM)
     own = tok // 4
-    kernel = functools.partial(layer_kernel, n, steps, heads, doc_lengths.shape[0])
+    kernel = functools.partial(layer_kernel, n, gaps, heads, doc_lengths.shape[0])
     return pl.pallas_call(
         kernel,
         out_shape=jax.ShapeDtypeStruct((own, model), BF16),
-        in_specs=[vmem, smem, smem] + [vmem] * 7,
+        in_specs=[vmem, smem, smem] + [hbm] * 4 + [vmem] * 2 + [hbm],
         out_specs=vmem,
         scratch_shapes=[
+            pltpu.VMEM((tok, wide), BF16),
+            pltpu.VMEM((tok, wide), BF16),
+            pltpu.VMEM((tok, state), BF16),
+            pltpu.VMEM((tok, state), BF16),
+            pltpu.VMEM((wide, model), BF16),
+            pltpu.VMEM((LANES, tok), F32),
+            pltpu.SemaphoreType.DMA((5,)),
+            pltpu.VMEM((n, cap, 2 * state), BF16),
+            pltpu.VMEM((n, cap, 2 * state), BF16),
+            pltpu.SemaphoreType.DMA((n,)),
+            pltpu.SemaphoreType.DMA((n,)),
+            pltpu.SemaphoreType.DMA((n // 4, 4)),
             pltpu.VMEM((n, cap, aux), BF16),
             pltpu.VMEM((n, cap, wide), BF16),
             pltpu.VMEM((n, cap, wide), BF16),
             pltpu.VMEM((n, cap, aux), BF16),
             pltpu.VMEM((n, cap, wide), BF16),
             pltpu.VMEM((n, cap, wide), BF16),
-            pltpu.VMEM((steps, state + 16, wide), BF16),
-            pltpu.VMEM((steps, state + 16, wide), BF16),
+            pltpu.VMEM((state + 16, wide), BF16),
+            pltpu.VMEM((state + 16, wide), BF16),
+            pltpu.VMEM((steps, state + 16, wide // 2), BF16),
+            pltpu.VMEM((steps, state + 16, wide // 2), BF16),
+            pltpu.VMEM((state, wide // 2), BF16),
+            pltpu.VMEM((state, wide // 2), BF16),
             pltpu.VMEM((tok, wide), BF16),
             pltpu.VMEM((tok, wide), BF16),
             pltpu.VMEM((tok, wide), BF16),
@@ -418,8 +566,8 @@
             pltpu.VMEM((own, model), BF16),
             pltpu.SemaphoreType.DMA((3, n)),
             pltpu.SemaphoreType.DMA((3, n)),
-            pltpu.SemaphoreType.DMA((steps,)),
-            pltpu.SemaphoreType.DMA((steps,)),
+            pltpu.SemaphoreType.DMA((steps + 2,)),
+            pltpu.SemaphoreType.DMA((steps + 2,)),
             pltpu.SemaphoreType.DMA((6,)),
             pltpu.SemaphoreType.DMA((6,)),
         ],
@@ -435,8 +583,8 @@
         gate_in,
         b_input,
         c_input,
-        small,
-        norm_gain.reshape(1, wide),
+        log_decay.T,
+        norm_gain,
         out_weight,
     )
 

time: 86.8 us -> 79.3 us (0.914)
  Pallas kernels: 79.1 us -> 71.9 us
    pallas_call x1, Pallas kernels: 79.1 us -> 71.9 us  [body(): pl.pallas_call(kernel, out_shape=jax.ShapeDtypeStruct((own, model), BF16)...]
    unnamed x13 -> x17, local copies, waits for them, and re-layouts: 5.67 us -> 7.08 us
where the time goes in v2:
time: 79.3 us; the launch traced here: 79 us
  Pallas kernels  71.9 us (91%)
  local copies, waits for them, and re-layouts  7.08 us (9%)
    pallas_call x1, Pallas kernels, body(): pl.pallas_call(kernel, out_shape=jax.ShapeDtypeStruct((own, model), BF16)...  71.9 us
    unnamed x17, local copies, waits for them, and re-layouts  7.08 us

profile of v2, /device:TPU:27, one launch (start us, length us, event | category | flops | bytes accessed | tf_op | source)
XLA Modules:
  0.0 79.0 jit_solution(9729291210460250716)
XLA Ops:
  0.0 0.0 copy-start
  0.0 1.1 %copy-done = bf16[512,768]{1,0:T(8,128)(2,1)S(1)} copy-done((bf16[512,768]{1,0:T(8,128)(2,1)S(1)}, bf16[512,768]{1,0:T(8,128)(2,1)}, u32[]{:S(2)}) %copy-start) | copy-done | bytes 786456
  1.1 0.0 copy-start.1
  1.1 0.9 %copy-done.1 = bf16[512,128]{1,0:T(8,128)(2,1)S(1)} copy-done((bf16[512,128]{1,0:T(8,128)(2,1)S(1)}, bf16[512,128]{1,0:T(8,128)(2,1)}, u32[]{:S(2)}) %copy-start.1) | copy-done | bytes 131096
  2.0 0.0 copy-start.2
  2.0 0.9 %copy-done.2 = bf16[512,128]{1,0:T(8,128)(2,1)S(1)} copy-done((bf16[512,128]{1,0:T(8,128)(2,1)S(1)}, bf16[512,128]{1,0:T(8,128)(2,1)}, u32[]{:S(2)}) %copy-start.2) | copy-done | bytes 131096
  2.9 0.0 copy-start.3
  2.9 0.7 copy-done.3
  3.7 0.0 copy-start.4
  3.7 0.7 copy-done.4
  4.3 0.0 copy-start.5
  4.4 0.7 copy-done.5
  5.0 0.0 copy-start.6
  5.0 0.7 copy-done.6
  5.7 0.0 copy-start.7
  5.7 0.7 copy-done.7
  6.3 71.9 %layer.1 = bf16[128,1536]{1,0:T(8,128)(2,1)S(1)} custom-call(s32[1,512]{1,0:T(1,128)S(1)} %bitcast.3, s32[4]{0:T(128)S(1)} %copy-done.6, f32[12]{0:T(128)S(1)} %copy-done.7, bf16[512,768]{1,0:T(8,128)(2,1)S(1)} %copy-done, bf16[512,768]{1,0:T(8,128)(2,1)} %z_hbm.1, bf16[512,128]{1,0:T(8,128)(2,1)S(1)} %copy-done.1, bf16[512,128]{1,0:T(8,128)(2,1)S(1)} %copy-done.2, ...), custom_call_target="tpu_custom_call" | custom-call | tf_op jit(solution)/shard_map/layer/pallas_call | solution.py:524
  78.3 0.7 copy.12
Async XLA Ops:
  0.0 1.1 %copy-start = (bf16[512,768]{1,0:T(8,128)(2,1)S(1)}, bf16[512,768]{1,0:T(8,128)(2,1)}, u32[]{:S(2)}) copy-start(bf16[512,768]{1,0:T(8,128)(2,1)} %x_hbm.1) | copy-start | bytes 2359300
  1.1 0.9 %copy-start.1 = (bf16[512,128]{1,0:T(8,128)(2,1)S(1)}, bf16[512,128]{1,0:T(8,128)(2,1)}, u32[]{:S(2)}) copy-start(bf16[512,128]{1,0:T(8,128)(2,1)} %b_hbm.1) | copy-start | bytes 393220
  2.0 0.9 %copy-start.2 = (bf16[512,128]{1,0:T(8,128)(2,1)S(1)}, bf16[512,128]{1,0:T(8,128)(2,1)}, u32[]{:S(2)}) copy-start(bf16[512,128]{1,0:T(8,128)(2,1)} %c_hbm.1) | copy-start | bytes 393220
  2.9 0.7 copy-start.3
  3.7 0.7 copy-start.4
  4.3 0.7 copy-start.5
  5.0 0.7 copy-start.6
  5.7 0.7 copy-start.7

commit v3 on v2

--- a/solution.py
+++ b/solution.py
@@ -68,6 +68,8 @@
     state_recv,
     last_send,
     last_recv,
+    entry_ref,
+    opening_ref,
     xs_ref,
     xw_ref,
     zs_ref,
@@ -286,7 +288,7 @@
     running_t = running.T
     closing = running[tok - 1 : tok]
     weight = jnp.exp(closing - running) * jnp.where(doc_col == doc_last, 1.0, 0.0)
-    entry = jnp.exp(running) * jnp.where(doc_col == doc_before, 1.0, 0.0)
+    opening_ref[...] = jnp.exp(running) * jnp.where(doc_col == doc_before, 1.0, 0.0)
     through = jnp.exp(closing) * jnp.where(doc_last == doc_before, 1.0, 0.0)
     allowed = low & (doc_col == doc_line)
     gm_ref[...] = jnp.where(allowed, dot(cs_ref[...], b_t), 0.0)
@@ -314,11 +316,11 @@
         tail = ref[state:].astype(F32)
         return ref[0:state].astype(F32), tail[0:1] + tail[1:2]
 
-    def pair_copy(which, src, dst):
+    def pair_copy(which, src, dst, sem):
         return pltpu.make_async_remote_copy(
             src_ref=src,
             dst_ref=dst,
-            send_sem=state_out_sem.at[which],
+            send_sem=state_out_sem.at[sem],
             recv_sem=state_in_sem.at[which],
             device_id={"seq": pair_peer},
             device_id_type=MESH,
@@ -328,8 +330,8 @@
         return pltpu.make_async_remote_copy(
             src_ref=state_send.at[step],
             dst_ref=state_recv.at[step],
-            send_sem=state_out_sem.at[2 + step],
-            recv_sem=state_in_sem.at[2 + step],
+            send_sem=state_out_sem.at[3 + step],
+            recv_sem=state_in_sem.at[3 + step],
             device_id={"seq": (me + 2 * gaps[step]) % n},
             device_id_type=MESH,
         )
@@ -376,14 +378,19 @@
         for j in range(pairs * stage // stages, pairs * (stage + 1) // stages):
             inner(j)
 
-    first_copy = pair_copy(0, pair_send, pair_recv)
-    last_copy = pair_copy(1, last_send, last_recv)
-    fill(pair_send, held, kept)
-    first_copy.start()
+    part = wide // 2
+
+    def half_copy(which):
+        return pair_copy(which, pair_send.at[which], pair_recv.at[which], which)
+
+    last_copy = pair_copy(2, last_send, last_recv, 2)
+    for i in range(2):
+        fill(pair_send.at[i], held[:, i * part : (i + 1) * part], kept[:, i * part : (i + 1) * part])
+    half_copy(1 - column).start()
+    half_copy(column).start()
     inner_of(0)
-    first_copy.wait_recv()
-    part = wide // 2
-    other, other_kept = read(pair_recv)
+    half_copy(column).wait_recv()
+    other, other_kept = read(pair_recv.at[column])
 
     def ordered(own_one, other_one):
         early = jnp.where(column == 0, own_one, other_one)
@@ -393,8 +400,8 @@
     def my_half(values):
         return jnp.where(column == 0, values[:, 0:part], values[:, part:])
 
-    early, late = ordered(my_half(held), my_half(other))
-    early_kept, late_kept = ordered(my_half(kept), my_half(other_kept))
+    early, late = ordered(my_half(held), other)
+    early_kept, late_kept = ordered(my_half(kept), other_kept)
     sent, sent_kept = late + late_kept * early, late_kept * early_kept
     for step in range(len(gaps)):
         state_start(step, sent, sent_kept)
@@ -407,26 +414,27 @@
     last_copy.start()
     inner_of(stages - 1)
     wait_in(2, send_z, recv_z)
-    zs_ref[...] = dot(unperm, packed_rows(recv_z)).astype(BF16)
+    gate = dot(unperm, packed_rows(recv_z))
+    zs_ref[...] = gate / (1.0 + jnp.exp(-gate))
     last_copy.wait_recv()
     early, late = ordered(last_send[...].astype(F32), last_recv[...].astype(F32))
-    held = jnp.concatenate([early, late], axis=1)
-    other, other_kept = read(pair_recv)
-    held = jnp.where(column == 0, held, other + other_kept * held)
-    entry_state = held.astype(BF16)
-    mixed_ref[...] += dot(cs_ref[...], entry_state) * jnp.concatenate(
-        [spread(entry, j) for j in range(pairs)], axis=1
-    )
-
-    def gate_half(where):
-        rows = pl.ds(pl.multiple_of(where * half, half), half)
-        gate = zs_ref[rows, :].astype(F32)
-        gated = mixed_ref[rows, :] * (gate / (1.0 + jnp.exp(-gate)))
+    half_copy(1 - column).wait_recv()
+    for i, came in enumerate((early, late)):
+        other, other_kept = read(pair_recv.at[i])
+        came = jnp.where(column == 0, came, other + other_kept * came)
+        entry_ref[:, i * part : (i + 1) * part] = came.astype(BF16)
+
+    def gate_rows(where_side, where_core):
+        at = where_side * 2 + where_core
+        rows = pl.ds(pl.multiple_of(at * own, own), own)
+        share = opening_ref[rows, :]
+        share = jnp.concatenate([spread(share, j) for j in range(pairs)], axis=1)
+        gated = mixed_ref[rows, :] + dot(cs_ref[rows, :], entry_ref[...]) * share
+        gated = gated * zs_ref[rows, :]
         gs_ref[rows, :] = (gated * gain_ref[...].reshape(1, wide)).astype(BF16)
         squares = jnp.sum(gated * gated, axis=1, keepdims=True)
-        squares = jnp.broadcast_to(squares, (half, LANES)).T[0:8]
-        for i in range(2):
-            sq_ref[pl.ds(2 * where + i, 1)] = squares[None, :, i * own : (i + 1) * own]
+        squares = jnp.broadcast_to(squares, (own, LANES)).T[0:8]
+        sq_ref[pl.ds(at, 1)] = squares[None]
 
     def partial(where_side, where_core):
         at = (where_side * 2 + where_core) * own
@@ -445,21 +453,23 @@
     loads[4].wait()
     copies = [head_copy(i, a_send.at[i], a_recv.at[i], core_peer) for i in range(2)]
     across = head_copy(2, y_send, y_recv, side_peer)
-    gate_half(1 - side)
+    gate_rows(1 - side, 1 - core)
     a_send[0] = partial(1 - side, 1 - core).astype(BF16)
     copies[0].start()
+    gate_rows(1 - side, core)
     passing = partial(1 - side, core)
     copies[0].wait_recv()
     y_send[...] = (passing + a_recv[0].astype(F32)).astype(BF16)
     across.start()
-    gate_half(side)
+    gate_rows(side, 1 - core)
+    a_send[1] = partial(side, 1 - core).astype(BF16)
+    copies[1].start()
+    gate_rows(side, core)
     sq_copies = [
         head_copy(2 + k, sq_ref.at[(hd + k) % 4], sq_recv.at[k], (hd + k) % 4) for k in range(1, 4)
     ]
     for copy in sq_copies:
         copy.start()
-    a_send[1] = partial(side, 1 - core).astype(BF16)
-    copies[1].start()
     total = partial(side, core)
     for copy in sq_copies:
         copy.wait_recv()
@@ -481,7 +491,8 @@
             bc_share(i, p).wait_send()
 
     mine(shared_out)
-    first_copy.wait_send()
+    for i in range(2):
+        half_copy(i).wait_send()
     last_copy.wait_send()
     for step in range(len(gaps)):
 
@@ -545,15 +556,17 @@
             pltpu.VMEM((n, cap, aux), BF16),
             pltpu.VMEM((n, cap, wide), BF16),
             pltpu.VMEM((n, cap, wide), BF16),
-            pltpu.VMEM((state + 16, wide), BF16),
-            pltpu.VMEM((state + 16, wide), BF16),
+            pltpu.VMEM((2, state + 16, wide // 2), BF16),
+            pltpu.VMEM((2, state + 16, wide // 2), BF16),
             pltpu.VMEM((steps, state + 16, wide // 2), BF16),
             pltpu.VMEM((steps, state + 16, wide // 2), BF16),
             pltpu.VMEM((state, wide // 2), BF16),
             pltpu.VMEM((state, wide // 2), BF16),
+            pltpu.VMEM((state, wide), BF16),
+            pltpu.VMEM((tok, LANES), F32),
             pltpu.VMEM((tok, wide), BF16),
             pltpu.VMEM((tok, wide), BF16),
-            pltpu.VMEM((tok, wide), BF16),
+            pltpu.VMEM((tok, wide), F32),
             pltpu.VMEM((tok, state), BF16),
             pltpu.VMEM((tok, tok), F32),
             pltpu.VMEM((tok, wide), F32),
@@ -566,13 +579,13 @@
             pltpu.VMEM((own, model), BF16),
             pltpu.SemaphoreType.DMA((3, n)),
             pltpu.SemaphoreType.DMA((3, n)),
-            pltpu.SemaphoreType.DMA((steps + 2,)),
-            pltpu.SemaphoreType.DMA((steps + 2,)),
+            pltpu.SemaphoreType.DMA((steps + 3,)),
+            pltpu.SemaphoreType.DMA((steps + 3,)),
             pltpu.SemaphoreType.DMA((6,)),
             pltpu.SemaphoreType.DMA((6,)),
         ],
         compiler_params=pltpu.CompilerParams(
-            collective_id=0, has_side_effects=True, vmem_limit_bytes=52 * 1024 * 1024
+            collective_id=0, has_side_effects=True, vmem_limit_bytes=61 * 1024 * 1024
         ),
         name="layer",
     )(

time: 79.3 us -> 71.8 us (0.905)
  local copies, waits for them, and re-layouts: 7.08 us -> 1.77 us
  Pallas kernels: 71.9 us -> 69.8 us
    unnamed x17 -> x1, local copies, waits for them, and re-layouts: 7.08 us -> 1.77 us
    pallas_call x1, Pallas kernels: 71.9 us -> 69.8 us  [body(): pl.pallas_call(kernel, out_shape=jax.ShapeDtypeStruct((own, model), BF16)...]
where the time goes in v3:
time: 71.8 us; the launch traced here: 71.6 us
  Pallas kernels  69.8 us (97%)
  local copies, waits for them, and re-layouts  1.77 us (2%)
    pallas_call x1, Pallas kernels, body(): pl.pallas_call(kernel, out_shape=jax.ShapeDtypeStruct((own, model), BF16)...  69.8 us
    unnamed x1, local copies, waits for them, and re-layouts  1.77 us

profile of v3, /device:TPU:27, one launch (start us, length us, event | category | flops | bytes accessed | tf_op | source)
XLA Modules:
  0.0 71.6 jit_solution(5945617363229227883)
XLA Ops:
  0.0 69.8 %layer.1 = bf16[128,1536]{1,0:T(8,128)(2,1)} custom-call(s32[1,512]{1,0:T(1,128)} %bitcast.3, s32[4]{0:T(128)} %doc_ref.1, f32[12]{0:T(128)} %skip_ref.1, bf16[512,768]{1,0:T(8,128)(2,1)} %x_hbm.1, bf16[512,768]{1,0:T(8,128)(2,1)} %z_hbm.1, bf16[512,128]{1,0:T(8,128)(2,1)} %b_hbm.1, bf16[512,128]{1,0:T(8,128)(2,1)} %c_hbm.1, bf16[12,512]{1,0:T(8,128)(2,1)} %bitcast.2, ...), custom_call_target="tpu_custom_call" | custom-call | tf_op jit(solution)/shard_map/layer/pallas_call | solution.py:535
  69.9 1.8 %copy.12 = bf16[128,1536]{1,0:T(8,128)(2,1)} copy(bf16[128,1536]{1,0:T(8,128)(2,1)} %layer.1) | data formatting | bytes 786432

commit v4 on v3

--- a/solution.py
+++ b/solution.py
@@ -238,7 +238,7 @@
     recv_x[0] = send_x[0]
     loads[3].wait()
     send_z[...] = by_slot(dot(perm, z_ref[...]))
-    start_all(2, send_z, recv_z, 1, n)
+    start_all(2, send_z, recv_z, 1, n // 2)
     recv_z[0] = send_z[0]
 
     first_place = me * tok
@@ -405,6 +405,8 @@
     sent, sent_kept = late + late_kept * early, late_kept * early_kept
     for step in range(len(gaps)):
         state_start(step, sent, sent_kept)
+        if step == 0:
+            start_all(2, send_z, recv_z, n // 2, n)
         inner_of(1 + step)
         came, came_kept = state_finish(step)
         if step > 0:

time: 71.8 us -> 72.4 us (level)
  no operation moved by 1% of the time
where the time goes in v4:
time: 72.4 us; the launch traced here: 71.8 us
  Pallas kernels  70 us (97%)
  local copies, waits for them, and re-layouts  1.77 us (2%)
    pallas_call x1, Pallas kernels, body(): pl.pallas_call(kernel, out_shape=jax.ShapeDtypeStruct((own, model), BF16)...  70 us
    unnamed x1, local copies, waits for them, and re-layouts  1.77 us

profile of v4, /device:TPU:27, one launch (start us, length us, event | category | flops | bytes accessed | tf_op | source)
XLA Modules:
  0.0 71.8 jit_solution(11295864929256091566)
XLA Ops:
  0.0 70.0 %layer.1 = bf16[128,1536]{1,0:T(8,128)(2,1)} custom-call(s32[1,512]{1,0:T(1,128)} %bitcast.3, s32[4]{0:T(128)} %doc_ref.1, f32[12]{0:T(128)} %skip_ref.1, bf16[512,768]{1,0:T(8,128)(2,1)} %x_hbm.1, bf16[512,768]{1,0:T(8,128)(2,1)} %z_hbm.1, bf16[512,128]{1,0:T(8,128)(2,1)} %b_hbm.1, bf16[512,128]{1,0:T(8,128)(2,1)} %c_hbm.1, bf16[12,512]{1,0:T(8,128)(2,1)} %bitcast.2, ...), custom_call_target="tpu_custom_call" | custom-call | tf_op jit(solution)/shard_map/layer/pallas_call | solution.py:537
  70.0 1.8 %copy.12 = bf16[128,1536]{1,0:T(8,128)(2,1)} copy(bf16[128,1536]{1,0:T(8,128)(2,1)} %layer.1) | data formatting | bytes 786432

commit v5 on v3

--- a/solution.py
+++ b/solution.py
@@ -357,9 +357,9 @@
     def inner(j):
         cols = slice(j * LANES, (j + 1) * LANES)
         skip = jnp.where(left, skip_ref[2 * j], skip_ref[2 * j + 1])
-        for t0 in range(0, tok, half):
-            rows = slice(t0, t0 + half)
-            upto = t0 + half
+        for t0 in range(0, tok, own):
+            rows = slice(t0, t0 + own)
+            upto = t0 + own
             keys = xs_ref[0:upto, cols]
             sums = []
             for h in (2 * j, 2 * j + 1):

time: 71.8 us -> 71.9 us (level)
  no operation moved by 1% of the time
where the time goes in v5:
time: 71.9 us; the launch traced here: 71.7 us
  Pallas kernels  69.9 us (97%)
  local copies, waits for them, and re-layouts  1.77 us (2%)
    pallas_call x1, Pallas kernels, body(): pl.pallas_call(kernel, out_shape=jax.ShapeDtypeStruct((own, model), BF16)...  69.9 us
    unnamed x1, local copies, waits for them, and re-layouts  1.77 us

profile of v5, /device:TPU:27, one launch (start us, length us, event | category | flops | bytes accessed | tf_op | source)
XLA Modules:
  0.0 71.7 jit_solution(7859824102889478074)
XLA Ops:
  0.0 69.9 %layer.1 = bf16[128,1536]{1,0:T(8,128)(2,1)} custom-call(s32[1,512]{1,0:T(1,128)} %bitcast.3, s32[4]{0:T(128)} %doc_ref.1, f32[12]{0:T(128)} %skip_ref.1, bf16[512,768]{1,0:T(8,128)(2,1)} %x_hbm.1, bf16[512,768]{1,0:T(8,128)(2,1)} %z_hbm.1, bf16[512,128]{1,0:T(8,128)(2,1)} %b_hbm.1, bf16[512,128]{1,0:T(8,128)(2,1)} %c_hbm.1, bf16[12,512]{1,0:T(8,128)(2,1)} %bitcast.2, ...), custom_call_target="tpu_custom_call" | custom-call | tf_op jit(solution)/shard_map/layer/pallas_call | solution.py:535
  69.9 1.8 %copy.12 = bf16[128,1536]{1,0:T(8,128)(2,1)} copy(bf16[128,1536]{1,0:T(8,128)(2,1)} %layer.1) | data formatting | bytes 786432
